TPU v7x, 128 devices: a whole 4x4x4 slice. The times are simulated.
128 devices in a mesh: story: 16 (over z, y), plan: 8 (over x, core).
Axes of the slice: x: 4, y: 4, z: 4, core: 2. Of those that a mesh axis runs over, the one named last changes fastest.
Arguments:
- schur_blocks: float32 [16, 8, 4, 1, 6, 128, 128], P('story', 'plan'), may hold values from -4 to 19, as said below
- off_pattern: int32 [16, 8, 4, 1, 2, 2], P('story', 'plan'), may hold values from 0 to 3, as said below
- face_owner: int32 [16, 8, 4, 1], P('story', 'plan'), may hold values from 0 to 1, as said below
- residual: float32 [16, 8, 4, 1, 64, 512], P('story', 'plan'), may hold values from -6 to 6
- coarse_basis: float32 [16, 8, 4, 1, 30, 512], P('story', 'plan'), may hold values from -0.25 to 0.25
- coarse_inverse: float32 [768, 768], replicated, may hold values from -1 to 9, as said below
Outputs:
- averaged: float32 [16, 8, 4, 1, 64, 512], P('story', 'plan')
- coarse_part: float32 [16, 8, 4, 1, 64, 512], P('story', 'plan')
Inputs may be any that keep to these rules, and one draw needn't show every extreme that they name: `off_pattern`: the two entries of a pair differ, and both sides of a face carry the same pairs; entries on sides without a face are arbitrary. `face_owner`: each face has exactly one owner among its two sharers; sides without a face hold 0. `schur_blocks`: each side's piece is symmetric positive definite. `coarse_inverse`: Symmetric.
All inputs are finite; a program needn't handle non-finite values.
Results may differ from a plain program's by a relative error of at most 0.0003.
Values sent between devices are 32-bit elements; how exact they have to be, the bound alone decides.
A program may use at most 128 MiB of HBM per device.

v0:
```python
import jax
import jax.numpy as jnp
from jax import lax
from jax.experimental import pallas as pl
from jax.experimental.pallas import tpu as pltpu
from jax.sharding import PartitionSpec as P

ITERS = 6
DAMPING = 0.3
BLK = 128
NBLK = 4
RHS = 64
FD = 512
CPD = 6
KC = 30
STORIES = 16
PLANS = 8
ROW = PLANS * CPD
NCOARSE = STORIES * ROW
MESH = pl.DeviceIdType.MESH
F32 = jnp.float32
BF16 = jnp.bfloat16


def iota(shape, dim):
    return lax.broadcasted_iota(jnp.int32, shape, dim)


def split(value):
    high = value.astype(BF16)
    return high, (value - high.astype(F32)).astype(BF16)


def dot(left, right):
    return jnp.dot(left, right, preferred_element_type=F32)


def dot_last(left, right):
    return lax.dot_general(left, right, (((1,), (1,)), ((), ())), preferred_element_type=F32)


def product(value, high, low, dot=dot):
    rows = value.shape[0]
    first, second = split(value)
    both = dot(jnp.concatenate([first, second], axis=0), high)
    return both[:rows] + both[rows:] + dot(first, low)


def fill(table, first, second):
    zero = jnp.zeros_like(first)
    for a, left in enumerate((zero, first, first.T)):
        for b, right in enumerate((zero, second, second.T)):
            table[3 * a + b] = left + right


def choice(pattern, side, q, t):
    index = 0
    for k in range(2):
        row, column = pattern[k, 0, side], pattern[k, 1, side]
        plain = jnp.where((row == q) & (column == t), 1, 0)
        turned = jnp.where((row == t) & (column == q), 2, 0)
        index = 3 * index + plain + turned
    return index


def place(pattern, side, table, diagonal, scales, high, low):
    for q in range(NBLK):
        for t in range(NBLK):
            if q == t:
                block = diagonal[q]
            else:
                block = table[choice(pattern, side, q, t)]
                if scales is not None:
                    block = block * scales[t]
            here = (pl.ds(q * BLK, BLK), pl.ds(t * BLK, BLK))
            high[here], low[here] = split(block)


def places(dof):
    group = (dof * 43) >> 8
    storey = jnp.where(group == 1, -1, jnp.where(group == 2, 1, 0))
    column = jnp.where(group == 4, 1, jnp.where(group == 3, PLANS - 1, 0))
    return storey, column, dof - CPD * group


def scatter(plan, shift):
    dof, lane = iota((32, 256), 0), iota((32, 256), 1)
    storey, column, member = places(dof)
    target = (storey + shift) * ROW + ((plan + column) & (PLANS - 1)) * CPD + member
    return jnp.where((lane == target) & (dof < KC), 1.0, 0.0)


def gather(plan):
    lane = iota((1, STORIES * 32), 1)
    dof = lane & 31
    storey, column, member = places(dof)
    storey = storey + (lane >> 5)
    target = storey * ROW + ((plan + column) & (PLANS - 1)) * CPD + member
    target = jnp.where((dof < KC) & (storey >= 0) & (storey < STORIES), target, -1)
    return jnp.where(iota((NCOARSE, STORIES * 32), 0) == target, 1.0, 0.0).astype(BF16)


def kernel(
    schur, pattern_far, owner_far, residual, basis, inverse,
    averaged, coarse_part,
    pattern, owner, raw, rows, local, slab, table, high, low, ready_high, ready_low,
    pack_out, pack_in, coupling_in, product_out, product_in, product_own, basis_in,
    wide, owned_high, owned_low, weight_high, weight_low, basis_pack, flag, flags,
    sent_first, got_first, sent_second, got_second,
    load_sem, face_send, face_recv, back_send, back_recv,
    send_flag, recv_flag, send_first, recv_first, send_second, recv_second, near, middle, far, last,
):
    story, plan = lax.axis_index("story"), lax.axis_index("plan")
    odd = lax.rem(plan, 2)
    step = 1 - 2 * odd
    in_side = (1 - odd, 3)
    out_side = (odd, 2)
    sides = (out_side[0], out_side[1], in_side[0], in_side[1])
    in_device = ((lax.rem(story + step + STORIES, STORIES), plan), (story, lax.rem(plan + 1, PLANS)))
    out_device = (
        (lax.rem(story - step + STORIES, STORIES), plan),
        (story, lax.rem(plan + PLANS - 1, PLANS)),
    )
    plan_peers = [(story, lax.rem(plan + r, PLANS)) for r in (4, 3, 5, 2, 6, 1, 7)]

    barrier = pltpu.get_barrier_semaphore()

    def around(distance):
        peers = [
            (story >= distance, (lax.rem(story + STORIES - distance, STORIES), plan)),
            (story < STORIES - distance, (lax.rem(story + distance, STORIES), plan)),
        ]
        if distance <= PLANS // 2:
            for r in sorted({distance, PLANS - distance}):
                peers.append((None, (story, lax.rem(plan + r, PLANS))))
        return peers

    def announce(semaphore, distance):
        for condition, peer in around(distance):
            def signal(peer=peer):
                pl.semaphore_signal(semaphore, inc=1, device_id=peer, device_id_type=MESH)

            if condition is None:
                signal()
            else:
                pl.when(condition)(signal)

    def hear(semaphore, distance):
        count = 0
        for condition, _ in around(distance):
            count = count + (1 if condition is None else jnp.where(condition, 1, 0))
        pl.semaphore_wait(semaphore, count)

    announce(barrier, 1)

    small = (
        pltpu.make_async_copy(pattern_far, pattern, load_sem.at[10]),
        pltpu.make_async_copy(owner_far, owner, load_sem.at[11]),
    )
    loads = []
    for k in range(4):
        loads.append(pltpu.make_async_copy(schur.at[sides[k]], raw.at[k], load_sem.at[k]))
        loads.append(pltpu.make_async_copy(residual.at[sides[k]], rows.at[k], load_sem.at[4 + k]))
    loads.append(pltpu.make_async_copy(basis, local, load_sem.at[8]))
    lowest = jnp.clip(story - 2, 0, STORIES - 5)
    loads.append(
        pltpu.make_async_copy(
            inverse.at[pl.ds(pl.multiple_of(lowest * ROW, 8), 5 * ROW)], slab, load_sem.at[9]
        )
    )
    for load in loads[:4]:
        load.start()

    line, lane = iota((BLK, BLK), 0), iota((BLK, BLK), 1)
    upper, equal = line <= lane, line == lane

    def diagonal_of(block):
        return jnp.sum(jnp.where(equal, block, 0.0), axis=0, keepdims=True)

    def to_sharer(f, m, source, target):
        return pltpu.make_async_remote_copy(
            src_ref=source, dst_ref=target, send_sem=face_send.at[f, m], recv_sem=face_recv.at[f, m],
            device_id=out_device[f], device_id_type=MESH,
        )

    def exchange(peers, source, target, send_sem, recv_sem):
        copies = []
        for r, peer in enumerate(peers):
            copies.append(
                pltpu.make_async_remote_copy(
                    src_ref=source(peer), dst_ref=target, send_sem=send_sem.at[r],
                    recv_sem=recv_sem.at[r], device_id=peer, device_id_type=MESH,
                )
            )
            copies[-1].start()
        return copies

    hear(barrier, 1)
    couplings = [
        to_sharer(f, 1, schur.at[out_side[f], pl.ds(NBLK, 2)], coupling_in.at[f]) for f in range(2)
    ]
    packs = [to_sharer(f, 0, pack_out.at[f], pack_in.at[f]) for f in range(2)]
    products = [to_sharer(f, 2, product_out.at[f], product_in.at[f]) for f in range(2)]
    bases = [to_sharer(f, 3, basis.at[out_side[f]], basis_in.at[f]) for f in range(2)]
    exists = jnp.where(odd == 0, story < STORIES - 1, story > 0)
    leaves = jnp.where(odd == 0, story > 0, story < STORIES - 1)

    def when(condition, f, action):
        if f == 0:
            pl.when(condition)(action)
        else:
            action()

    for f in range(2):
        when(leaves, f, couplings[f].start)
    for load in list(small) + loads[4:]:
        load.start()

    for f in range(2):
        loads[2 * f].wait()
        for h in range(2):
            first, second = raw[f, 2 * h], raw[f, 2 * h + 1]
            pack_out[f, h * BLK : (h + 1) * BLK] = jnp.where(upper, first, second)
            pack_out[f, 2 * BLK + h : 2 * BLK + h + 1] = diagonal_of(second)
        pack_out[f, 2 * BLK + 2 : 2 * BLK + 8] = jnp.zeros((6, BLK), F32)
        when(leaves, f, packs[f].start)
        when(leaves, f, bases[f].start)
    announce(near, 1)

    for copy in small:
        copy.wait()
    mine = [owner[0, in_side[f]].astype(F32) for f in range(2)]
    for f in range(2):
        flag[f : f + 1] = jnp.full((1, BLK), mine[f], F32)
    flag[2:8] = jnp.zeros((6, BLK), F32)
    flags[plan] = flag[...]

    for k in range(4):
        if k >= 2:
            loads[2 * k].wait()
        loads[2 * k + 1].wait()
        fill(table, raw[k, NBLK], raw[k, NBLK + 1])
        place(pattern, sides[k], table, [raw[k, n] for n in range(NBLK)], None, high, low)
        target = product_out.at[k] if k < 2 else product_own.at[k - 2]
        target[...] = product(rows[k], high[...], low[...])
        if k < 2:
            when(leaves, k, products[k].start)
    hear(near, 1)
    announce(middle, 2)

    present = (jnp.where(story > 0, 1.0, 0.0), jnp.where(story < STORIES - 1, 1.0, 0.0), 1.0, 1.0)
    loads[8].wait()
    wide[...] = jnp.zeros_like(wide)

    def widen(source, s, target):
        for n in range(NBLK):
            wide[target, 0:KC, n * BLK : (n + 1) * BLK] = source[s, pl.ds(n, KC, stride=NBLK)]

    for s in range(4):
        widen(local, s, s)
        basis_high, basis_low = split(wide[s] * present[s])
        here = pl.ds(s * FD, FD)
        basis_pack[:, here] = jnp.concatenate(
            [basis_high, basis_high, basis_low, jnp.zeros_like(basis_low)], axis=0
        )

    loads[9].wait()
    slab_high, slab_low = split(jnp.concatenate([slab[...], jnp.zeros((16, NCOARSE), F32)], axis=0))
    columns = dot(jnp.concatenate([slab_high, slab_low], axis=0), gather(plan)).astype(BF16)
    hear(middle, 2)
    announce(far, 4)
    noted = exchange(plan_peers, lambda peer: flag, flags.at[plan], send_flag, recv_flag)
    def sweeps(start, f):
        values = start
        for _ in range(ITERS - 1):
            values = start + product(values, ready_high[f], ready_low[f])
        return values

    def both_sweeps(start):
        values = start
        for _ in range(ITERS - 1):
            values = [start[f] + product(values[f], ready_high[f], ready_low[f]) for f in range(2)]
        return values

    owned_high[...] = jnp.zeros_like(owned_high)
    owned_low[...] = jnp.zeros_like(owned_low)
    scaled = [None, None]
    for f in (1, 0):
        when(exists, f, packs[f].wait_recv)
        when(exists, f, couplings[f].wait_recv)
        diagonal, scales = [], []
        for h in range(2):
            first, second = raw[2 + f, 2 * h], raw[2 + f, 2 * h + 1]
            packed = jnp.where(upper, first, second) + pack_in[f, h * BLK : (h + 1) * BLK]
            turned = packed.T
            second_diagonal = diagonal_of(second) + pack_in[f, 2 * BLK + h : 2 * BLK + h + 1]
            scales += [-DAMPING / diagonal_of(packed), -DAMPING / second_diagonal]
            diagonal.append(
                jnp.where(equal, 1.0 - DAMPING, jnp.where(upper, packed, turned) * scales[-2])
            )
            diagonal.append(
                jnp.where(equal, 1.0 - DAMPING, jnp.where(upper, turned, packed) * scales[-1])
            )
        fill(
            table,
            raw[2 + f, NBLK] + coupling_in[f, 0],
            raw[2 + f, NBLK + 1] + coupling_in[f, 1],
        )
        place(pattern, in_side[f], table, diagonal, scales, ready_high.at[f], ready_low.at[f])
        scaled[f] = jnp.concatenate(scales, axis=1)
        when(exists, f, bases[f].wait_recv)
        widen(basis_in, f, 4 + f)
        share = wide[in_side[f]] * mine[f] + wide[4 + f] * (1.0 - mine[f])
        share = sweeps(-share * scaled[f], f)
        if f == 0:
            share = jnp.where(exists, share, 0.0)
        share_high, share_low = split(share)
        for n in range(2):
            here = (pl.ds(64 * n + 32 * f, 32), pl.ds(f * FD, FD))
            owned_high[here], owned_low[here] = share_high, share_low

    right_side = []
    for f in range(2):
        when(exists, f, products[f].wait_recv)
        right_side.append(product_own[f] + product_in[f])
    right_side[0] = jnp.where(exists, right_side[0], 0.0)
    values = jnp.concatenate(right_side, axis=1)
    contribution = product(values, owned_high[...], owned_low[...], dot_last)
    left = iota((RHS // 2, BLK), 1) < 64
    packed = jnp.where(left, contribution[: RHS // 2], contribution[RHS // 2 :])
    sent_first[...] = packed
    firsts = exchange(plan_peers, lambda peer: sent_first, got_first.at[plan], send_first, recv_first)

    got_first[plan] = packed
    hear(far, 4)
    announce(last, 8)
    for copy in noted:
        copy.wait_recv()
    height = story - lowest
    chosen = []
    for p in range(PLANS):
        for f in range(2):
            kept = jnp.concatenate([flags[p, f : f + 1]] * 2, axis=1)
            other = scatter(p, height + 1 - 2 * (p % 2)) if f == 0 else scatter(p + 1, height)
            chosen.append((scatter(p, height) * kept + other * (1.0 - kept)).astype(BF16))
    chosen = jnp.concatenate(chosen, axis=0)
    weight_high[...] = dot(chosen, columns[:256]).astype(BF16)
    weight_low[...] = dot(chosen, columns[256:]).astype(BF16)
    solved = both_sweeps([-right_side[f] * scaled[f] for f in range(2)])
    solved[0] = jnp.where(exists, solved[0], 0.0)
    for f in range(2):
        averaged[in_side[f]] = solved[f]

    def to_owner(f):
        return pltpu.make_async_remote_copy(
            src_ref=averaged.at[in_side[f]], dst_ref=averaged.at[out_side[f]],
            send_sem=back_send.at[f], recv_sem=back_recv.at[f],
            device_id=in_device[f], device_id_type=MESH,
        )

    backs = [to_owner(f) for f in range(2)]
    when(exists, 0, backs[0].start)

    @pl.when(jnp.logical_not(leaves))
    def _():
        averaged[out_side[0]] = jnp.zeros((RHS, FD), F32)


    for copy in firsts:
        copy.wait_recv()
    halves = ([], [])
    for p in range(0, PLANS, 2):
        first, second = got_first[p], got_first[p + 1]
        halves[0].append(jnp.where(left, first, pltpu.roll(second, 64, 1)))
        halves[1].append(jnp.where(left, pltpu.roll(first, 64, 1), second))
    gathered = jnp.concatenate([jnp.concatenate(half, axis=1) for half in halves], axis=0)
    hear(last, 8)
    quarter = iota((16, BLK), 1) >> 5
    seconds = []
    for n in range(STORIES // 4):
        if n % 2 == 0:
            here = pl.ds(n * BLK, 2 * BLK)
            coarse = product(gathered, weight_high[:, here], weight_low[:, here])
        tile = coarse[:, (n % 2) * BLK : (n % 2 + 1) * BLK]
        turned = [pltpu.roll(tile, 32 * g, 1) if g else tile for g in range(4)]
        for q in range(4):
            message = turned[(3 - q) % 4][48:64]
            for g in range(3):
                message = jnp.where(quarter == g, turned[(g - q) % 4][16 * g : 16 * g + 16], message)
            sent_second[4 * n + q] = message
        if n % 2 == 0:
            continue
        for i in range(4 * n - 4, 4 * n + 4):
            seconds.append(
                pltpu.make_async_remote_copy(
                    src_ref=sent_second.at[i], dst_ref=got_second.at[story], send_sem=send_second.at[i],
                    recv_sem=recv_second.at[story], device_id=(i, plan), device_id_type=MESH,
                )
            )
            pl.when(story != i)(seconds[-1].start)

    def arrival(i):
        return pltpu.make_async_remote_copy(
            src_ref=sent_second.at[i], dst_ref=got_second.at[i], send_sem=send_second.at[i],
            recv_sem=recv_second.at[i], device_id=(i, plan), device_id_type=MESH,
        )

    backs[1].start()
    got_second[story] = sent_second[story]
    for i in range(STORIES):
        pl.when(story != i)(arrival(i).wait_recv)
    total = got_second[0]
    for i in range(1, STORIES):
        total = total + got_second[i]
    parts = [total] + [pltpu.roll(total, BLK - 32 * g, 1) for g in range(1, 4)]
    needed = jnp.concatenate(parts, axis=0)
    needed = jnp.where(iota((RHS, BLK), 1) < 32, needed, 0.0)
    needed_high, needed_low = split(needed)
    needed_high, needed_low = needed_high.astype(F32), needed_low.astype(F32)
    operand = needed_high + pltpu.roll(needed_low, 32, 1) + pltpu.roll(needed_high, 64, 1)
    operand = operand.astype(BF16)
    for s in range(4):
        coarse_part[s] = dot(operand, basis_pack[:, s * FD : (s + 1) * FD])

    for copies in (packs, couplings, products, bases):
        for f in range(2):
            when(leaves, f, copies[f].wait_send)
    for copy in noted + firsts:
        copy.wait_send()
    for i in range(STORIES):
        pl.when(story != i)(seconds[i].wait_send)
    for f in range(2):
        when(exists, f, backs[f].wait_send)
        when(leaves, f, backs[f].wait_recv)


def store(averaged, coarse_part, averaged_out, coarse_part_out, sem):
    copies = []
    for s in range(4):
        copies.append(pltpu.make_async_copy(averaged.at[s], averaged_out.at[s], sem.at[0, s]))
        copies.append(pltpu.make_async_copy(coarse_part.at[s], coarse_part_out.at[s], sem.at[1, s]))
    for copy in copies:
        copy.start()
    for copy in copies:
        copy.wait()


def on_device(schur_blocks, off_pattern, face_owner, residual, coarse_basis, coarse_inverse):
    hbm = pl.BlockSpec(memory_space=pltpu.HBM)
    operands = [
        pltpu.with_memory_space_constraint(operand, pltpu.HBM)
        for operand in (
            schur_blocks.reshape(4, 6, BLK, BLK),
            off_pattern.reshape(4, 2, 2).transpose(1, 2, 0),
            face_owner.reshape(1, 4),
            residual.reshape(4, RHS, FD),
            coarse_basis.reshape(4, KC * NBLK, BLK),
            coarse_inverse,
        )
    ]
    vmem = pl.BlockSpec(memory_space=pltpu.VMEM)
    dma = pltpu.SemaphoreType.DMA
    out = pltpu.VMEM((4, RHS, FD), F32)
    averaged, coarse_part = pl.pallas_call(
        kernel,
        out_shape=(out, out),
        in_specs=[hbm] * 6,
        out_specs=(vmem, vmem),
        scratch_shapes=[
            pltpu.SMEM((2, 2, 4), jnp.int32),
            pltpu.SMEM((1, 4), jnp.int32),
            pltpu.VMEM((4, 6, BLK, BLK), F32),
            pltpu.VMEM((4, RHS, FD), F32),
            pltpu.VMEM((4, KC * NBLK, BLK), F32),
            pltpu.VMEM((5 * ROW, NCOARSE), F32),
            pltpu.VMEM((9, BLK, BLK), F32),
            pltpu.VMEM((FD, FD), BF16),
            pltpu.VMEM((FD, FD), BF16),
            pltpu.VMEM((2, FD, FD), BF16),
            pltpu.VMEM((2, FD, FD), BF16),
            pltpu.VMEM((2, 2 * BLK + 8, BLK), F32),
            pltpu.VMEM((2, 2 * BLK + 8, BLK), F32),
            pltpu.VMEM((2, 2, BLK, BLK), F32),
            pltpu.VMEM((2, RHS, FD), F32),
            pltpu.VMEM((2, RHS, FD), F32),
            pltpu.VMEM((2, RHS, FD), F32),
            pltpu.VMEM((2, KC * NBLK, BLK), F32),
            pltpu.VMEM((6, 32, FD), F32),
            pltpu.VMEM((BLK, 2 * FD), BF16),
            pltpu.VMEM((BLK, 2 * FD), BF16),
            pltpu.VMEM((PLANS * 64, STORIES * 32), BF16),
            pltpu.VMEM((PLANS * 64, STORIES * 32), BF16),
            pltpu.VMEM((BLK, 4 * FD), BF16),
            pltpu.VMEM((8, BLK), F32),
            pltpu.VMEM((PLANS, 8, BLK), F32),
            pltpu.VMEM((RHS // 2, BLK), F32),
            pltpu.VMEM((PLANS, RHS // 2, BLK), F32),
            pltpu.VMEM((STORIES, 16, BLK), F32),
            pltpu.VMEM((STORIES, 16, BLK), F32),
            dma((12,)),
            dma((2, 4)),
            dma((2, 4)),
            dma((2,)),
            dma((2,)),
            dma((PLANS - 1,)),
            dma((PLANS - 1,)),
            dma((PLANS - 1,)),
            dma((PLANS - 1,)),
            dma((STORIES,)),
            dma((STORIES,)),
            pltpu.SemaphoreType.REGULAR,
            pltpu.SemaphoreType.REGULAR,
            pltpu.SemaphoreType.REGULAR,
            pltpu.SemaphoreType.REGULAR,
        ],
        compiler_params=pltpu.CompilerParams(
            collective_id=0, has_side_effects=True, vmem_limit_bytes=40 * 1024 * 1024
        ),
    )(*operands)
    free = pl.BlockSpec(memory_space=pl.ANY)
    out = pltpu.HBM((4, RHS, FD), F32)
    averaged, coarse_part = pl.pallas_call(
        store,
        out_shape=(out, out),
        in_specs=[free, free],
        out_specs=(free, free),
        scratch_shapes=[dma((2, 4))],
    )(*[pltpu.with_memory_space_constraint(value, pltpu.VMEM) for value in (averaged, coarse_part)])
    shape = (1, 1, 4, 1, RHS, FD)
    return averaged.reshape(shape), coarse_part.reshape(shape)


def solution(mesh):
    in_specs = (
        P("story", "plan", None, None, None, None, None),
        P("story", "plan", None, None, None, None),
        P("story", "plan", None, None),
        P("story", "plan", None, None, None, None),
        P("story", "plan", None, None, None, None),
        P(),
    )
    out_specs = (
        P("story", "plan", None, None, None, None),
        P("story", "plan", None, None, None, None),
    )
    return jax.shard_map(
        on_device, mesh=mesh, in_specs=in_specs, out_specs=out_specs, check_vma=False
    )
```

profile of v0, /device:TPU:1, one launch (start us, length us, event | category | flops | bytes accessed | tf_op | source)
XLA Modules:
  0.0 27.9 jit_solution(6412198708484347579)
XLA Ops:
  0.6 26.2 %shard_map.77 = (f32[4,64,512]{2,1,0:T(8,128)S(1)}, f32[4,64,512]{2,1,0:T(8,128)S(1)}) custom-call(f32[4,6,128,128]{3,2,1,0:T(8,128)} %bitcast.13, s32[2,2,4]{2,1,0:T(2,128)} %bitcast.16, s32[1,4]{1,0:T(1,128)} %bitcast.17, f32[4,64,512]{2,1,0:T(8,128)} %bitcast.14, f32[4,120,128]{2,1,0:T(8,128)} %bitcast.15, f32[768,768]{1,0:T(8,128)} %inverse.1), custom_call_target="tpu_custom_call" | custom-call | tf_op jit(solution)/shard_map/pallas_call | solution.py:464
  26.9 1.0 %shard_map.78 = (f32[4,64,512]{2,1,0:T(8,128)}, f32[4,64,512]{2,1,0:T(8,128)}) custom-call(f32[4,64,512]{2,1,0:T(8,128)S(1)} %get-tuple-element.6.averaged, f32[4,64,512]{2,1,0:T(8,128)S(1)} %get-tuple-element.7.coarse_part), custom_call_target="tpu_custom_call" | custom-call | tf_op jit(solution)/shard_map/pallas_call | solution.py:522
where the time goes:
time: 28.2 us; the launch traced here: 27.9 us
  Pallas kernels  27.3 us (97%)
  between operations  0.64 us (2%)
    pallas_call x1, Pallas kernels, on_device(): pl.pallas_call(kernel, out_shape=(out, out), in_specs=[hbm] * 6, out_spec...  26.2 us
    pallas_call x1, Pallas kernels, on_device(): pl.pallas_call(store, out_shape=(out, out), in_specs=[free, free], out_sp...  1.03 us

commit v1 on v0

--- a/solution.py
+++ b/solution.py
@@ -102,10 +102,10 @@
 
 def kernel(
     schur, pattern_far, owner_far, residual, basis, inverse,
-    averaged, coarse_part,
+    averaged, needed_part, basis_pack,
     pattern, owner, raw, rows, local, slab, table, high, low, ready_high, ready_low,
     pack_out, pack_in, coupling_in, product_out, product_in, product_own, basis_in,
-    wide, owned_high, owned_low, weight_high, weight_low, basis_pack, flag, flags,
+    wide, owned_high, owned_low, weight_high, weight_low, flag, flags,
     sent_first, got_first, sent_second, got_second,
     load_sem, face_send, face_recv, back_send, back_recv,
     send_flag, recv_flag, send_first, recv_first, send_second, recv_second, near, middle, far, last,
@@ -319,13 +319,16 @@
             here = (pl.ds(64 * n + 32 * f, 32), pl.ds(f * FD, FD))
             owned_high[here], owned_low[here] = share_high, share_low
 
-    right_side = []
-    for f in range(2):
+    right_side, contribution = [None, None], 0.0
+    for f in (1, 0):
         when(exists, f, products[f].wait_recv)
-        right_side.append(product_own[f] + product_in[f])
-    right_side[0] = jnp.where(exists, right_side[0], 0.0)
-    values = jnp.concatenate(right_side, axis=1)
-    contribution = product(values, owned_high[...], owned_low[...], dot_last)
+        right_side[f] = product_own[f] + product_in[f]
+        if f == 0:
+            right_side[f] = jnp.where(exists, right_side[f], 0.0)
+        here = pl.ds(f * FD, FD)
+        contribution = contribution + product(
+            right_side[f], owned_high[:, here], owned_low[:, here], dot_last
+        )
     left = iota((RHS // 2, BLK), 1) < 64
     packed = jnp.where(left, contribution[: RHS // 2], contribution[RHS // 2 :])
     sent_first[...] = packed
@@ -418,10 +421,7 @@
     needed_high, needed_low = split(needed)
     needed_high, needed_low = needed_high.astype(F32), needed_low.astype(F32)
     operand = needed_high + pltpu.roll(needed_low, 32, 1) + pltpu.roll(needed_high, 64, 1)
-    operand = operand.astype(BF16)
-    for s in range(4):
-        coarse_part[s] = dot(operand, basis_pack[:, s * FD : (s + 1) * FD])
-
+    needed_part[...] = operand.astype(BF16)
     for copies in (packs, couplings, products, bases):
         for f in range(2):
             when(leaves, f, copies[f].wait_send)
@@ -434,13 +434,14 @@
         when(leaves, f, backs[f].wait_recv)
 
 
-def store(averaged, coarse_part, averaged_out, coarse_part_out, sem):
-    copies = []
-    for s in range(4):
-        copies.append(pltpu.make_async_copy(averaged.at[s], averaged_out.at[s], sem.at[0, s]))
-        copies.append(pltpu.make_async_copy(coarse_part.at[s], coarse_part_out.at[s], sem.at[1, s]))
+def store(averaged, needed, basis_pack, averaged_out, coarse_part_out, result, sem):
+    copies = [pltpu.make_async_copy(averaged.at[s], averaged_out.at[s], sem.at[0, s]) for s in range(4)]
     for copy in copies:
         copy.start()
+    for s in range(4):
+        result[s] = dot(needed[...], basis_pack[:, s * FD : (s + 1) * FD])
+        copies.append(pltpu.make_async_copy(result.at[s], coarse_part_out.at[s], sem.at[1, s]))
+        copies[-1].start()
     for copy in copies:
         copy.wait()
 
@@ -461,11 +462,11 @@
     vmem = pl.BlockSpec(memory_space=pltpu.VMEM)
     dma = pltpu.SemaphoreType.DMA
     out = pltpu.VMEM((4, RHS, FD), F32)
-    averaged, coarse_part = pl.pallas_call(
+    averaged, needed, basis_pack = pl.pallas_call(
         kernel,
-        out_shape=(out, out),
+        out_shape=(out, pltpu.VMEM((RHS, BLK), BF16), pltpu.VMEM((BLK, 4 * FD), BF16)),
         in_specs=[hbm] * 6,
-        out_specs=(vmem, vmem),
+        out_specs=(vmem, vmem, vmem),
         scratch_shapes=[
             pltpu.SMEM((2, 2, 4), jnp.int32),
             pltpu.SMEM((1, 4), jnp.int32),
@@ -490,7 +491,6 @@
             pltpu.VMEM((BLK, 2 * FD), BF16),
             pltpu.VMEM((PLANS * 64, STORIES * 32), BF16),
             pltpu.VMEM((PLANS * 64, STORIES * 32), BF16),
-            pltpu.VMEM((BLK, 4 * FD), BF16),
             pltpu.VMEM((8, BLK), F32),
             pltpu.VMEM((PLANS, 8, BLK), F32),
             pltpu.VMEM((RHS // 2, BLK), F32),
@@ -522,10 +522,11 @@
     averaged, coarse_part = pl.pallas_call(
         store,
         out_shape=(out, out),
-        in_specs=[free, free],
+        in_specs=[free, vmem, vmem],
         out_specs=(free, free),
-        scratch_shapes=[dma((2, 4))],
-    )(*[pltpu.with_memory_space_constraint(value, pltpu.VMEM) for value in (averaged, coarse_part)])
+        scratch_shapes=[pltpu.VMEM((4, RHS, FD), F32), dma((2, 4))],
+        compiler_params=pltpu.CompilerParams(vmem_limit_bytes=16 * 1024 * 1024),
+    )(*[pltpu.with_memory_space_constraint(value, pltpu.VMEM) for value in (averaged, needed, basis_pack)])
     shape = (1, 1, 4, 1, RHS, FD)
     return averaged.reshape(shape), coarse_part.reshape(shape)
 

time: 28.2 us -> 28 us (level)
  no operation moved by 1% of the time
where the time goes in v1:
time: 28 us; the launch traced here: 27.7 us
  Pallas kernels  27.1 us (97%)
  between operations  0.64 us (2%)
    pallas_call x1, Pallas kernels, on_device(): pl.pallas_call(kernel, out_shape=(out, pltpu.VMEM((RHS, BLK), BF16), pltp...  26 us
    pallas_call x1, Pallas kernels, on_device(): pl.pallas_call(store, out_shape=(out, out), in_specs=[free, vmem, vmem],...  1.03 us

profile of v1, /device:TPU:1, one launch (start us, length us, event | category | flops | bytes accessed | tf_op | source)
XLA Modules:
  0.0 27.7 jit_solution(4883194183827198305)
XLA Ops:
  0.6 26.0 %shard_map.77 = (f32[4,64,512]{2,1,0:T(8,128)S(1)}, bf16[64,128]{1,0:T(8,128)(2,1)S(1)}, bf16[128,2048]{1,0:T(8,128)(2,1)S(1)}) custom-call(f32[4,6,128,128]{3,2,1,0:T(8,128)} %bitcast.13, s32[2,2,4]{2,1,0:T(2,128)} %bitcast.16, s32[1,4]{1,0:T(1,128)} %bitcast.17, f32[4,64,512]{2,1,0:T(8,128)} %bitcast.14, f32[4,120,128]{2,1,0:T(8,128)} %bitcast.15, ...), custom_call_target="tpu_custom_call" | custom-call | tf_op jit(solution)/shard_map/pallas_call | solution.py:465
  26.7 1.0 %shard_map.78 = (f32[4,64,512]{2,1,0:T(8,128)}, f32[4,64,512]{2,1,0:T(8,128)}) custom-call(f32[4,64,512]{2,1,0:T(8,128)S(1)} %get-tuple-element.7.averaged, bf16[64,128]{1,0:T(8,128)(2,1)S(1)} %get-tuple-element.8.needed, bf16[128,2048]{1,0:T(8,128)(2,1)S(1)} %get-tuple-element.9.basis_pack), custom_call_target="tpu_custom_call" | custom-call | tf_op jit(solution)/shard_map/pallas_call | solution.py:522

commit v2 on v1

--- a/solution.py
+++ b/solution.py
@@ -410,6 +410,13 @@
 
     backs[1].start()
     got_second[story] = sent_second[story]
+    for copies in (packs, couplings, products, bases):
+        for f in range(2):
+            when(leaves, f, copies[f].wait_send)
+    for copy in noted + firsts:
+        copy.wait_send()
+    for i in range(STORIES):
+        pl.when(story != i)(seconds[i].wait_send)
     for i in range(STORIES):
         pl.when(story != i)(arrival(i).wait_recv)
     total = got_second[0]
@@ -422,13 +429,6 @@
     needed_high, needed_low = needed_high.astype(F32), needed_low.astype(F32)
     operand = needed_high + pltpu.roll(needed_low, 32, 1) + pltpu.roll(needed_high, 64, 1)
     needed_part[...] = operand.astype(BF16)
-    for copies in (packs, couplings, products, bases):
-        for f in range(2):
-            when(leaves, f, copies[f].wait_send)
-    for copy in noted + firsts:
-        copy.wait_send()
-    for i in range(STORIES):
-        pl.when(story != i)(seconds[i].wait_send)
     for f in range(2):
         when(exists, f, backs[f].wait_send)
         when(leaves, f, backs[f].wait_recv)

time: 28 us -> 28 us (level)
  no operation moved by 1% of the time
where the time goes in v2:
time: 28 us; the launch traced here: 27.6 us
  Pallas kernels  27 us (96%)
  between operations  0.64 us (2%)
    pallas_call x1, Pallas kernels, on_device(): pl.pallas_call(kernel, out_shape=(out, pltpu.VMEM((RHS, BLK), BF16), pltp...  26 us
    pallas_call x1, Pallas kernels, on_device(): pl.pallas_call(store, out_shape=(out, out), in_specs=[free, vmem, vmem],...  1.03 us

profile of v2, /device:TPU:1, one launch (start us, length us, event | category | flops | bytes accessed | tf_op | source)
XLA Modules:
  0.0 27.6 jit_solution(1812114520572227842)
XLA Ops:
  0.6 26.0 %shard_map.77 = (f32[4,64,512]{2,1,0:T(8,128)S(1)}, bf16[64,128]{1,0:T(8,128)(2,1)S(1)}, bf16[128,2048]{1,0:T(8,128)(2,1)S(1)}) custom-call(f32[4,6,128,128]{3,2,1,0:T(8,128)} %bitcast.13, s32[2,2,4]{2,1,0:T(2,128)} %bitcast.16, s32[1,4]{1,0:T(1,128)} %bitcast.17, f32[4,64,512]{2,1,0:T(8,128)} %bitcast.14, f32[4,120,128]{2,1,0:T(8,128)} %bitcast.15, ...), custom_call_target="tpu_custom_call" | custom-call | tf_op jit(solution)/shard_map/pallas_call | solution.py:465
  26.6 1.0 %shard_map.78 = (f32[4,64,512]{2,1,0:T(8,128)}, f32[4,64,512]{2,1,0:T(8,128)}) custom-call(f32[4,64,512]{2,1,0:T(8,128)S(1)} %get-tuple-element.7.averaged, bf16[64,128]{1,0:T(8,128)(2,1)S(1)} %get-tuple-element.8.needed, bf16[128,2048]{1,0:T(8,128)(2,1)S(1)} %get-tuple-element.9.basis_pack), custom_call_target="tpu_custom_call" | custom-call | tf_op jit(solution)/shard_map/pallas_call | solution.py:522

commit v3 on v2

--- a/solution.py
+++ b/solution.py
@@ -435,9 +435,8 @@
 
 
 def store(averaged, needed, basis_pack, averaged_out, coarse_part_out, result, sem):
-    copies = [pltpu.make_async_copy(averaged.at[s], averaged_out.at[s], sem.at[0, s]) for s in range(4)]
-    for copy in copies:
-        copy.start()
+    copies = [pltpu.make_async_copy(averaged, averaged_out, sem.at[0, 0])]
+    copies[0].start()
     for s in range(4):
         result[s] = dot(needed[...], basis_pack[:, s * FD : (s + 1) * FD])
         copies.append(pltpu.make_async_copy(result.at[s], coarse_part_out.at[s], sem.at[1, s]))

time: 28 us -> 28 us (level)
  no operation moved by 1% of the time
where the time goes in v3:
time: 28 us; the launch traced here: 27.6 us
  Pallas kernels  27 us (96%)
  between operations  0.64 us (2%)
    pallas_call x1, Pallas kernels, on_device(): pl.pallas_call(kernel, out_shape=(out, pltpu.VMEM((RHS, BLK), BF16), pltp...  26 us
    pallas_call x1, Pallas kernels, on_device(): pl.pallas_call(store, out_shape=(out, out), in_specs=[free, vmem, vmem],...  1.03 us

profile of v3, /device:TPU:1, one launch (start us, length us, event | category | flops | bytes accessed | tf_op | source)
XLA Modules:
  0.0 27.6 jit_solution(16278103470470159100)
XLA Ops:
  0.6 26.0 %shard_map.77 = (f32[4,64,512]{2,1,0:T(8,128)S(1)}, bf16[64,128]{1,0:T(8,128)(2,1)S(1)}, bf16[128,2048]{1,0:T(8,128)(2,1)S(1)}) custom-call(f32[4,6,128,128]{3,2,1,0:T(8,128)} %bitcast.13, s32[2,2,4]{2,1,0:T(2,128)} %bitcast.16, s32[1,4]{1,0:T(1,128)} %bitcast.17, f32[4,64,512]{2,1,0:T(8,128)} %bitcast.14, f32[4,120,128]{2,1,0:T(8,128)} %bitcast.15, ...), custom_call_target="tpu_custom_call" | custom-call | tf_op jit(solution)/shard_map/pallas_call | solution.py:464
  26.6 1.0 %shard_map.78 = (f32[4,64,512]{2,1,0:T(8,128)}, f32[4,64,512]{2,1,0:T(8,128)}) custom-call(f32[4,64,512]{2,1,0:T(8,128)S(1)} %get-tuple-element.7.averaged, bf16[64,128]{1,0:T(8,128)(2,1)S(1)} %get-tuple-element.8.needed, bf16[128,2048]{1,0:T(8,128)(2,1)S(1)} %get-tuple-element.9.basis_pack), custom_call_target="tpu_custom_call" | custom-call | tf_op jit(solution)/shard_map/pallas_call | solution.py:521
